TPU v7x, 32 devices: a whole 2x2x4 slice. The times are simulated.
32 devices in a mesh: seq: 8 (over z, x), tp: 2 (over y), grp: 2 (over core).
Axes of the slice: x: 2, y: 2, z: 4, core: 2. Of those that a mesh axis runs over, the one named last changes fastest.
Arguments:
- prefill_query: bfloat16 [2, 3072, 8192], P('grp', 'seq', 'tp'), may hold values from -6 to 6
- prefill_keys: bfloat16 [2, 3072, 1024], P('grp', 'seq', 'tp'), may hold values from -6 to 6
- prefill_values: bfloat16 [2, 3072, 1024], P('grp', 'seq', 'tp'), may hold values from -6 to 6
- decode_query: bfloat16 [2, 64, 4, 8192], P('grp', 'seq', None, 'tp'), may hold values from -6 to 6
- decode_keys: bfloat16 [2, 64, 4, 1024], P('grp', 'seq', None, 'tp'), may hold values from -6 to 6
- decode_values: bfloat16 [2, 64, 4, 1024], P('grp', 'seq', None, 'tp'), may hold values from -6 to 6
- page_table: int32 [2, 64, 16], P('grp', 'seq'), may hold values from 0 to 23
- context_lengths: int32 [2, 64], P('grp', 'seq'), may hold values from 1 to 2048
- check_rows: bfloat16 [8, 128], replicated, may hold values from -0.125 to 0.125
Outputs:
- prefill_out: bfloat16 [2, 3072, 8192], P('grp', 'seq', 'tp')
- decode_out: bfloat16 [2, 64, 4, 8192], P('grp', 'seq', None, 'tp')
- page_digest: float32 [2, 64, 8, 2048], P('grp', 'seq', None, 'tp')
Inputs may be any that keep to these rules, and one draw needn't show every extreme that they name: page_table[g, r, j] names the page of 128 tokens of prompt 1 - g that holds context tokens j * 128 to j * 128 + 127 of request r; pages may repeat. Request r reads its first context_lengths[g, r] context tokens.
All inputs are finite; a program needn't handle non-finite values.
Results may differ from a plain program's by a relative error of at most 0.014.
Values may be sent and summed in bfloat16 or wider, within the bound.
A program may use at most 128 MiB of HBM per device.

v0:
```python
import math

import jax
import jax.numpy as jnp
from jax import lax
from jax.sharding import PartitionSpec as P

HQ = 64
KVH = 8
HD = 128
PAGE = 128


neg_large = -1e30


def partner(shard, axis, apart):
    return lax.ppermute(shard, axis, [(i, i ^ 1 << apart) for i in range(lax.axis_size(axis))])


def for_sending(shard):
    return jax.tree.map(lambda a: a.astype(jnp.bfloat16) if a.dtype == jnp.float32 else a, shard)


def fold_block(folded, query_heads, key_block, value_block, columns, places):
    running_max, totals, summed = folded
    col_count = key_block.shape[0]
    kv_local = query_heads.shape[1]
    key_heads = key_block.reshape(col_count, kv_local, HD)
    value_heads = value_block.reshape(col_count, kv_local, HD)
    scores = jnp.einsum(
        "rkgd,ckd->kgrc", query_heads, key_heads, preferred_element_type=jnp.float32
    ) * (1.0 / math.sqrt(HD))
    allowed = columns[None, :] <= places[:, None]
    scores = jnp.where(allowed, scores, neg_large)
    new_max = jnp.maximum(running_max, jnp.max(scores, axis=-1))
    weights = jnp.where(allowed, jnp.exp(scores - new_max[..., None]), 0.0)
    fading = jnp.exp(running_max - new_max)
    totals = totals * fading + jnp.sum(weights, axis=-1)
    update = jnp.einsum(
        "kgrc,ckd->rkgd",
        weights.astype(jnp.bfloat16),
        value_heads,
        preferred_element_type=jnp.float32,
    )
    summed = summed * jnp.transpose(fading, (2, 0, 1))[..., None] + update
    return (new_max, totals, summed)


def attend_piece(folded, query_heads, key_rows, value_rows, columns, places):
    piece_rows = key_rows.shape[0]
    block_rows = math.gcd(1024, piece_rows)
    block_count = piece_rows // block_rows
    key_blocks = key_rows.reshape(block_count, block_rows, key_rows.shape[1])
    value_blocks = value_rows.reshape(block_count, block_rows, value_rows.shape[1])
    column_blocks = columns.reshape(block_count, block_rows)

    def advance(partial_state, member):
        key_block, value_block, column_block = member
        return (
            fold_block(partial_state, query_heads, key_block, value_block, column_block, places),
            None,
        )

    folded, ignored = lax.scan(advance, folded, (key_blocks, value_blocks, column_blocks))
    return folded


def split_halves(product):
    upper = product.astype(jnp.bfloat16)
    lower = (product - upper.astype(jnp.float32)).astype(jnp.bfloat16)
    return (upper, lower)


def remote_context(all_query, all_table, all_lengths, key_rows, value_rows, check_rows, first_page):
    asked_count, max_pages = all_table.shape
    row_count = key_rows.shape[0]
    kv_local = key_rows.shape[1] // HD
    own_pages = row_count // PAGE
    offsets = jnp.arange(PAGE, dtype=jnp.int32)
    page_hits = (
        all_table[:, :, None] == first_page + jnp.arange(own_pages, dtype=jnp.int32)[None, None, :]
    ).astype(jnp.float32)
    token_place = jnp.arange(max_pages, dtype=jnp.int32)[:, None] * PAGE + offsets[None, :]
    token_fits = (token_place[None] < all_lengths[:, None, None]).astype(jnp.float32)
    counts = jnp.einsum("ajp,ajo->apo", page_hits, token_fits).reshape(asked_count, row_count)
    key_heads = key_rows.reshape(row_count, kv_local, HD)
    value_heads = value_rows.reshape(row_count, kv_local, HD)
    scores = jnp.einsum(
        "askgd,ckd->askgc", all_query, key_heads, preferred_element_type=jnp.float32
    ) * (1.0 / math.sqrt(HD))
    live_mask = (counts > 0)[:, None, None, None, :]
    scores = jnp.where(live_mask, scores, neg_large)
    highest = jnp.max(scores, axis=-1)
    weights = jnp.where(live_mask, jnp.exp(scores - highest[..., None]), 0.0)
    repeats = counts[:, None, None, None, :]
    totals = jnp.sum(weights * repeats, axis=-1)
    weighted = lax.optimization_barrier(weights.astype(jnp.bfloat16)).astype(jnp.float32) * repeats
    weight_upper, weight_lower = split_halves(weighted)
    summed = jnp.einsum(
        "askgc,ckd->askgd", weight_upper, value_heads, preferred_element_type=jnp.float32
    )
    summed = summed + jnp.einsum(
        "askgc,ckd->askgd", weight_lower, value_heads, preferred_element_type=jnp.float32
    )
    paired = jnp.concatenate(
        [key_rows.reshape(row_count, kv_local, HD), value_rows.reshape(row_count, kv_local, HD)],
        axis=-1,
    )
    paired = paired.reshape(own_pages, PAGE, kv_local, 2 * HD)
    counted_checks = (
        counts.reshape(asked_count, own_pages, 1, PAGE) * check_rows.astype(jnp.float32)[None, None]
    )
    check_upper, check_lower = split_halves(counted_checks)
    digest = jnp.einsum("apco,poke->acke", check_upper, paired, preferred_element_type=jnp.float32)
    digest = digest + jnp.einsum(
        "apco,poke->acke", check_lower, paired, preferred_element_type=jnp.float32
    )
    return (highest, totals, summed, digest)


def finish(highest, totals, summed, asking, new_keys, new_values):
    requests, step_count, kv_local = (asking.shape[0], asking.shape[1], asking.shape[2])
    key_heads = new_keys.reshape(requests, step_count, kv_local, HD)
    value_heads = new_values.reshape(requests, step_count, kv_local, HD)
    fresh_scores = jnp.einsum(
        "rskgd,rjkd->rskgj", asking, key_heads, preferred_element_type=jnp.float32
    ) * (1.0 / math.sqrt(HD))
    step_order = jnp.arange(step_count, dtype=jnp.int32)
    causal = (step_order[None, :] <= step_order[:, None])[None, :, None, None, :]
    fresh_scores = jnp.where(causal, fresh_scores, neg_large)
    joint_max = jnp.maximum(highest, jnp.max(fresh_scores, axis=-1))
    fresh_weights = jnp.where(causal, jnp.exp(fresh_scores - joint_max[..., None]), 0.0)
    fading = jnp.exp(highest - joint_max)
    totals = totals * fading + jnp.sum(fresh_weights, axis=-1)
    summed = summed * fading[..., None] + jnp.einsum(
        "rskgj,rjkd->rskgd",
        fresh_weights.astype(jnp.bfloat16),
        value_heads,
        preferred_element_type=jnp.float32,
    )
    return (summed / totals[..., None]).reshape(requests, step_count, -1).astype(jnp.bfloat16)


def shards(
    prefill_query,
    prefill_keys,
    prefill_values,
    decode_query,
    decode_keys,
    decode_values,
    page_table,
    context_lengths,
    check_rows,
):
    groups = HQ // KVH
    key_rows = prefill_keys[0]
    value_rows = prefill_values[0]
    row_count = key_rows.shape[0]
    kv_local = key_rows.shape[1] // HD
    members = lax.axis_size("seq")
    own_index = lax.axis_index("seq")
    held_query = prefill_query[0]
    query_heads = held_query.reshape(row_count, kv_local, groups, HD)
    places = own_index * row_count + jnp.arange(row_count, dtype=jnp.int32)
    start_state = (
        jnp.full((kv_local, groups, row_count), neg_large, jnp.float32),
        jnp.zeros((kv_local, groups, row_count), jnp.float32),
        jnp.zeros((row_count, kv_local, groups, HD), jnp.float32),
    )
    shard_pair = (
        lax.all_gather(key_rows, "seq", axis=0, tiled=True),
        lax.all_gather(value_rows, "seq", axis=0, tiled=True),
    )
    piece_rows = shard_pair[0].shape[0]
    columns = jnp.arange(piece_rows, dtype=jnp.int32)
    running_max, totals, summed = attend_piece(
        start_state, query_heads, shard_pair[0], shard_pair[1], columns, places
    )
    held_out = (
        (summed / jnp.transpose(totals, (2, 0, 1))[..., None])
        .reshape(row_count, -1)
        .astype(jnp.bfloat16)
    )
    prefill_out = held_out[None]
    requests = decode_query.shape[1]
    step_count = decode_query.shape[2]
    asking = decode_query[0].reshape(requests, step_count, kv_local, groups, HD)
    own_table = page_table[0]
    lengths = context_lengths[0]
    sent_query, sent_table, sent_lengths = partner((decode_query[0], own_table, lengths), "grp", 0)
    all_query, all_table, all_lengths = (
        lax.all_gather(sent_query, "seq", axis=0, tiled=True),
        lax.all_gather(sent_table, "seq", axis=0, tiled=True),
        lax.all_gather(sent_lengths, "seq", axis=0, tiled=True),
    )
    asked_count = all_query.shape[0]
    partials = remote_context(
        all_query.reshape(asked_count, step_count, kv_local, groups, HD),
        all_table,
        all_lengths,
        key_rows,
        value_rows,
        check_rows,
        own_index * (row_count // PAGE),
    )
    by_owner = [member.reshape((members, requests) + member.shape[1:]) for member in partials]
    got_max, got_totals, got_summed, got_digest = (
        lax.all_to_all(
            by_owner[0].astype(jnp.bfloat16), "seq", split_axis=0, concat_axis=0, tiled=True
        ).astype(jnp.float32),
        lax.all_to_all(
            by_owner[1].astype(jnp.bfloat16), "seq", split_axis=0, concat_axis=0, tiled=True
        ).astype(jnp.float32),
        lax.all_to_all(
            by_owner[2].astype(jnp.bfloat16), "seq", split_axis=0, concat_axis=0, tiled=True
        ).astype(jnp.float32),
        lax.all_to_all(
            by_owner[3].astype(jnp.bfloat16), "seq", split_axis=0, concat_axis=0, tiled=True
        ).astype(jnp.float32),
    )
    overall = jnp.max(got_max, axis=0)
    fading = jnp.exp(got_max - overall[None])
    merged_totals = jnp.sum(got_totals * fading, axis=0)
    merged_summed = jnp.sum(got_summed * fading[..., None], axis=0)
    merged_digest = jnp.sum(got_digest, axis=0)
    highest, ctx_totals, ctx_summed, digest = (
        partner(for_sending(overall), "grp", 0).astype(overall.dtype),
        partner(for_sending(merged_totals), "grp", 0).astype(merged_totals.dtype),
        partner(for_sending(merged_summed), "grp", 0).astype(merged_summed.dtype),
        partner(for_sending(merged_digest), "grp", 0).astype(merged_digest.dtype),
    )
    decode_out = finish(highest, ctx_totals, ctx_summed, asking, decode_keys[0], decode_values[0])[
        None
    ]
    page_digest = digest.reshape(requests, digest.shape[1], -1)[None]
    return (prefill_out, decode_out, page_digest)


def solution(mesh):
    in_specs = (
        P("grp", "seq", "tp"),
        P("grp", "seq", "tp"),
        P("grp", "seq", "tp"),
        P("grp", "seq", None, "tp"),
        P("grp", "seq", None, "tp"),
        P("grp", "seq", None, "tp"),
        P("grp", "seq", None),
        P("grp", "seq"),
        P(),
    )
    out_specs = (P("grp", "seq", "tp"), P("grp", "seq", None, "tp"), P("grp", "seq", None, "tp"))
    return jax.shard_map(shards, mesh=mesh, in_specs=in_specs, out_specs=out_specs, check_vma=False)
```

profile of v0, /device:TPU:27, one launch (start us, length us, event | category | flops | bytes accessed | tf_op | source)
XLA Modules:
  0.0 452.8 jit_solution(7553813320777495735)
XLA Ops:
  7.2 0.7 collective-permute-start.2
  8.0 1.4 collective-permute-done.2
  11.4 1.1 concatenate.8
  12.5 1.1 concatenate.9
  13.8 0.7 convert_element_type.141
  14.5 1.2 dynamic-slice
  16.8 5.9 %all-reduce = s32[64]{0:T(128)S(1)} all-reduce(s32[64]{0:T(128)S(1)} %dynamic-update-slice), channel_id=1, replica_groups=mesh['seq'=8,'tp'=2,'grp'=2] {'seq'}, use_global_device_ids=true, to_apply=%add | all-reduce | flops 64 | bytes 512
  22.7 25.0 %all_gather.17 = s32[64,16]{1,0:T(8,128)S(1)} all-gather(s32[8,16]{1,0:T(8,128)S(1)} %collective-permute-done), channel_id=1, replica_groups=mesh['seq'=8,'tp'=2,'grp'=2] {'seq'}, dimensions={0}, use_global_device_ids=true | all-gather | bytes 4608 | tf_op jit(solution)/shard_map/all_gather | solution.py:194
  48.0 0.7 fusion.33
  48.7 1.7 fusion.22
  50.5 7.1 %all-to-all-start.3 = ((bf16[8,8,8,4,256]{4,2,3,1,0:T(8,128)(2,1)}), bf16[8,8,8,4,256]{4,2,3,1,0:T(8,128)(2,1)}, u32[]{:S(2)}, u32[]{:S(2)}) async-start(bf16[8,8,8,4,256]{4,2,3,1,0:T(8,128)(2,1)} %bitcast.32), calls=%async_computation.3 | async-start | bytes 2097152 | tf_op jit(solution)/shard_map/all_to_all | solution.py:218
  57.5 0.7 all-gather.10.cloned.1.call-update
  58.3 0.9 reshape_squeeze.21
  59.1 0.9 reshape_squeeze.22
  60.0 1.0 reshape_squeeze.24
  61.0 3.4 copy.134
  64.4 2.9 copy.136
  67.3 3.0 fusion.65
  70.3 0.7 copy.155
  71.0 11.8 %all-to-all-done.3 = bf16[8,8,8,4,256]{4,2,3,1,0:T(8,128)(2,1)} async-done(((bf16[8,8,8,4,256]{4,2,3,1,0:T(8,128)(2,1)}), bf16[8,8,8,4,256]{4,2,3,1,0:T(8,128)(2,1)}, u32[]{:S(2)}, u32[]{:S(2)}) %all-to-all-start.3) | async-done | bytes 1048608 | tf_op jit(solution)/shard_map/all_to_all | solution.py:218
  82.9 1.4 reduce_sum.61
  84.3 12.1 %collective-permute-start.6 = (bf16[8,8,4,256]{3,1,2,0:T(8,128)(2,1)S(1)}, bf16[8,8,4,256]{3,1,2,0:T(8,128)(2,1)S(1)}, u32[]{:S(2)}, u32[]{:S(2)}) collective-permute-start(bf16[8,8,4,256]{3,1,2,0:T(8,128)(2,1)S(1)} %reduce_sum.61), channel_id=1, source_target_pairs={{0,1},{1,0},{2,3},{3,2},{4,5},{5,4},{6,7},{7,6},{8,9},{9,8},{10,11... | collective-permute-start | bytes 393224 | tf_op jit(solution)/shard_map/ppermute | solution.py:18
  96.4 1.0 collective-permute-done.6
  97.4 0.7 convert.8
  98.1 3.9 reshape.164
  102.0 3.7 fusion.16
  105.7 6.1 %multiply_reduce_fusion = (bf16[64,4,4,8]{0,3,1,2:T(8,128)(2,1)S(1)}, bf16[64,4,4,8,384]{4,0,3,1,2:T(8,128)(2,1)}) fusion(f32[4,384,64,4,8]{1,2,4,3,0:T(8,128)S(1)} %get-tuple-element.181, f32[64,384]{1,0:T(8,128)S(1)} %get-tuple-element.169, f32[64,4,4,8]{0,3,1,2:T(8,128)S(1)} %get-tuple-element.180, pred[64,384]{1,0:T(8,128)(4,1)S(1)} %get-tuple-element.168), kind=kLoop, calls=%fused_computation.24 | loop fusion | flops 22011904 | bytes 19046400 | tf_op jit(solution)/shard_map/reduce_sum | solution.py:97
  112.1 0.9 reshape.171
  112.9 5.6 %all-to-all-start.1 = ((bf16[8,2,512]{2,1,0:T(2,128)(2,1)}), bf16[8,2,512]{2,1,0:T(2,128)(2,1)S(1)}, u32[]{:S(2)}, u32[]{:S(2)}) async-start(bf16[8,2,512]{2,1,0:T(2,128)(2,1)} %reshape.171), calls=%async_computation.1 | async-start | bytes 32768 | tf_op jit(solution)/shard_map/all_to_all | solution.py:209
  118.5 7.5 %fusion.15 = (bf16[64,4,4,8,384]{4,0,3,1,2:T(8,128)(2,1)S(1)}, bf16[64,4,4,8,384]{4,0,3,1,2:T(8,128)(2,1)}) fusion(bf16[64,4,4,8,384]{4,0,3,1,2:T(8,128)(2,1)} %get-tuple-element.175, f32[64,384]{1,0:T(8,128)S(1)} %get-tuple-element.169), kind=kLoop, calls=%fused_computation.27 | loop fusion | flops 18874368 | bytes 18972672 | tf_op jit(solution)/shard_map/convert_element_type | solution.py:70
  126.0 7.0 %fusion.18 = f32[4,64,4,8,128]{4,3,2,1,0:T(8,128)S(1)} fusion(bf16[64,4,4,8,384]{4,0,3,1,2:T(8,128)(2,1)} %get-tuple-element.177, bf16[384,4,128,1,1]{2,1,0,4,3:T(4,128)(2,1)} %bitcast.159), kind=kOutput, calls=%fused_computation.31 | convolution fusion | flops 805306368 | bytes 10878976 | tf_op jit(solution)/shard_map/askgc,ckd->askgd/dot_general | solution.py:103
  133.0 4.5 add_convert_fusion
  137.6 1.9 copy.146
  139.7 0.9 reshape.173
  140.5 5.4 %all-to-all-start.2 = ((bf16[8,2,512]{2,1,0:T(2,128)(2,1)}), bf16[8,2,512]{2,1,0:T(2,128)(2,1)S(1)}, u32[]{:S(2)}, u32[]{:S(2)}) async-start(bf16[8,2,512]{2,1,0:T(2,128)(2,1)} %reshape.173), calls=%async_computation.2 | async-start | bytes 32768 | tf_op jit(solution)/shard_map/all_to_all | solution.py:212
  146.4 1.4 collective-permute-start.4
  148.4 7.7 %all-to-all-start = ((bf16[8,8,4,4,8,128]{5,4,2,1,3,0:T(8,128)(2,1)}), bf16[8,8,4,4,8,128]{5,4,2,1,3,0:T(8,128)(2,1)}, u32[]{:S(2)}, u32[]{:S(2)}) async-start(bf16[8,8,4,4,8,128]{5,4,2,1,3,0:T(8,128)(2,1)} %copy.146), calls=%async_computation | async-start | bytes 4194304 | tf_op jit(solution)/shard_map/all_to_all | solution.py:215
  156.6 1.0 copy.150
  157.6 2.5 collective-permute-start.5
  161.2 0.7 copy.163
  161.9 0.7 copy.156
  162.7 56.1 %all-gather.10.cloned.1.call-done = bf16[1,3072,512]{2,1,0:T(8,128)(2,1)} async-done(((bf16[1,384,512]{2,1,0:T(8,128)(2,1)}), bf16[1,3072,512]{2,1,0:T(8,128)(2,1)}) %all-gather.10.cloned.1.call-update) | async-done | bytes 3145744 | tf_op jit(solution)/shard_map/all_gather | solution.py:173
  218.7 215.0 %while.15 = (s32[]{:T(128)}, f32[4,8,384]{2,1,0:T(8,128)S(1)}, f32[4,8,384]{2,1,0:T(8,128)S(1)}, f32[384,4,8,128]{0,3,2,1:T(8,128)}, s32[3,1024]{1,0:T(4,128)S(1...) while((s32[]{:T(128)}, f32[4,8,384]{2,1,0:T(8,128)S(1)}, ...), condition=%wide.region_3.4_spmd.clone, body=%wide.region_0.3_spmd.clone.sunk | while | flops 6611214848 | bytes 179584144 | solution.py:65
  219.0 2.7 constant_dynamic-slice_fusion.6
  221.7 1.5 copy.235
  223.2 20.1 %fusion.81 = (f32[4,8,384]{2,1,0:T(8,128)S(1)}, f32[4,1024,384,8]{2,1,3,0:T(8,128)}) fusion(pred[384,1024]{0,1:T(8,128)(4,1)S(1)} %broadcast_compare_fusion.3, bf16[1024,4,128,1]{0,2,3,1:T(8,128)(2,1)S(1)} %bitcast.152, bf16[384,4,8,128]{3,0,2,1:T(8,128)(2,1)} %get-tuple-element.279), kind=kOutput, calls=%fused_computation.3.clone.1 | convolution fusion | flops 3258961920 | bytes 54968320 | tf_op jit(solution)/shard_map/while/body/eval_jaxpr/rkgd,ckd->kgrc/dot_general | solution.py:31
  243.3 21.9 %fusion.83 = f32[4,8,384]{2,1,0:T(8,128)S(1)} fusion(f32[4,1024,384,8]{2,1,3,0:T(8,128)} %get-tuple-element.248, f32[4,8,384]{2,1,0:T(8,128)S(1)} %get-tuple-element.274, pred[384,1024]{0,1:T(8,128)(4,1)S(1)} %broadcast_compare_fusion.3), kind=kLoop, calls=%fused_computation.5.clone.1 | loop fusion | flops 62902272 | bytes 50823168 | tf_op jit(solution)/shard_map/while/body/eval_jaxpr/reduce_sum | solution.py:39
  265.8 23.3 %bitcast_add_fusion.3 = f32[384,4,8,128]{0,3,2,1:T(8,128)} fusion(f32[384,4,8,128]{0,3,2,1:T(8,128)} %get-tuple-element.265, f32[384,4,8]{0,2,1:T(8,128)S(1)} %get-tuple-element.249, pred[]{:T(512)S(6)} %compare.3, bf16[1024,4,128,1]{0,2,3,1:T(8,128)(2,1)S(1)} %bitcast.153, f32[4,1024,384,8]{2,1,3,0:T(8,128)} %get-tuple-element.248, ...), kind=kOutput, calls=%fused_computation.8.clone.1 | convolution fusion | flops 3288858624 | bytes 64454656 | tf_op jit(solution)/shard_map/while/body/eval_jaxpr/kgrc,ckd->rkgd/dot_general | solution.py:40
  289.5 2.7 constant_dynamic-slice_fusion.6
  292.1 1.5 copy.235
  293.6 20.1 %fusion.81 = (f32[4,8,384]{2,1,0:T(8,128)S(1)}, f32[4,1024,384,8]{2,1,3,0:T(8,128)}) fusion(pred[384,1024]{0,1:T(8,128)(4,1)S(1)} %broadcast_compare_fusion.3, bf16[1024,4,128,1]{0,2,3,1:T(8,128)(2,1)S(1)} %bitcast.152, bf16[384,4,8,128]{3,0,2,1:T(8,128)(2,1)} %get-tuple-element.279), kind=kOutput, calls=%fused_computation.3.clone.1 | convolution fusion | flops 3258961920 | bytes 54968320 | tf_op jit(solution)/shard_map/while/body/eval_jaxpr/rkgd,ckd->kgrc/dot_general | solution.py:31
  313.7 21.9 %fusion.83 = f32[4,8,384]{2,1,0:T(8,128)S(1)} fusion(f32[4,1024,384,8]{2,1,3,0:T(8,128)} %get-tuple-element.248, f32[4,8,384]{2,1,0:T(8,128)S(1)} %get-tuple-element.274, pred[384,1024]{0,1:T(8,128)(4,1)S(1)} %broadcast_compare_fusion.3), kind=kLoop, calls=%fused_computation.5.clone.1 | loop fusion | flops 62902272 | bytes 50823168 | tf_op jit(solution)/shard_map/while/body/eval_jaxpr/reduce_sum | solution.py:39
  336.3 25.1 %bitcast_add_fusion.3 = f32[384,4,8,128]{0,3,2,1:T(8,128)} fusion(f32[384,4,8,128]{0,3,2,1:T(8,128)} %get-tuple-element.265, f32[384,4,8]{0,2,1:T(8,128)S(1)} %get-tuple-element.249, pred[]{:T(512)S(6)} %compare.3, bf16[1024,4,128,1]{0,2,3,1:T(8,128)(2,1)S(1)} %bitcast.153, f32[4,1024,384,8]{2,1,3,0:T(8,128)} %get-tuple-element.248, ...), kind=kOutput, calls=%fused_computation.8.clone.1 | convolution fusion | flops 3288858624 | bytes 64454656 | tf_op jit(solution)/shard_map/while/body/eval_jaxpr/kgrc,ckd->rkgd/dot_general | solution.py:40
  361.7 2.7 constant_dynamic-slice_fusion.6
  364.4 1.5 copy.235
  365.9 20.1 %fusion.81 = (f32[4,8,384]{2,1,0:T(8,128)S(1)}, f32[4,1024,384,8]{2,1,3,0:T(8,128)}) fusion(pred[384,1024]{0,1:T(8,128)(4,1)S(1)} %broadcast_compare_fusion.3, bf16[1024,4,128,1]{0,2,3,1:T(8,128)(2,1)S(1)} %bitcast.152, bf16[384,4,8,128]{3,0,2,1:T(8,128)(2,1)} %get-tuple-element.279), kind=kOutput, calls=%fused_computation.3.clone.1 | convolution fusion | flops 3258961920 | bytes 54968320 | tf_op jit(solution)/shard_map/while/body/eval_jaxpr/rkgd,ckd->kgrc/dot_general | solution.py:31
  386.0 21.9 %fusion.83 = f32[4,8,384]{2,1,0:T(8,128)S(1)} fusion(f32[4,1024,384,8]{2,1,3,0:T(8,128)} %get-tuple-element.248, f32[4,8,384]{2,1,0:T(8,128)S(1)} %get-tuple-element.274, pred[384,1024]{0,1:T(8,128)(4,1)S(1)} %broadcast_compare_fusion.3), kind=kLoop, calls=%fused_computation.5.clone.1 | loop fusion | flops 62902272 | bytes 50823168 | tf_op jit(solution)/shard_map/while/body/eval_jaxpr/reduce_sum | solution.py:39
  408.6 25.1 %bitcast_add_fusion.3 = f32[384,4,8,128]{0,3,2,1:T(8,128)} fusion(f32[384,4,8,128]{0,3,2,1:T(8,128)} %get-tuple-element.265, f32[384,4,8]{0,2,1:T(8,128)S(1)} %get-tuple-element.249, pred[]{:T(512)S(6)} %compare.3, bf16[1024,4,128,1]{0,2,3,1:T(8,128)(2,1)S(1)} %bitcast.153, f32[4,1024,384,8]{2,1,3,0:T(8,128)} %get-tuple-element.248, ...), kind=kOutput, calls=%fused_computation.8.clone.1 | convolution fusion | flops 3288858624 | bytes 64454656 | tf_op jit(solution)/shard_map/while/body/eval_jaxpr/kgrc,ckd->rkgd/dot_general | solution.py:40
  433.7 2.5 multiply_reduce_fusion.1
  436.2 0.7 copy.221
  437.4 3.6 divide_convert_fusion
  441.0 2.9 copy.180
  443.9 1.5 divide_convert_fusion.1
  445.5 0.8 reshape.167
  (101 shorter events, 9.1 us)
Async XLA Ops:
  7.2 436.7 %copy-start = (bf16[1,8,4,512]{3,2,1,0:T(4,128)(2,1)S(1)}, bf16[1,8,4,512]{3,2,1,0:T(4,128)(2,1)}, u32[]{:S(2)}) copy-start(bf16[1,8,4,512]{3,2,1,0:T(4,128)(2,1)} %param.16) | copy-start | bytes 98308
  7.2 90.9 %all-gather.6.cloned.1.call-start = ((), (), s32[]{:S(2)}) async-start(), calls=%async_computation.4 | async-start | bytes 2359296 | tf_op jit(solution)/shard_map/all_gather | solution.py:193
  7.2 2.1 collective-permute-start.2
  9.3 0.7 copy-start.10
  10.1 152.6 %all-gather.8.cloned.1.call-start = ((), (), s32[]{:S(2)}) async-start(), calls=%async_computation.5 | async-start | bytes 3538944 | tf_op jit(solution)/shard_map/all_gather | solution.py:172
  10.8 5.7 %collective-permute-start.1 = (s32[8]{0:T(128)}, s32[8]{0:T(128)S(1)}, u32[]{:S(2)}, u32[]{:S(2)}) collective-permute-start(s32[8]{0:T(128)} %bitcast.170), channel_id=1, source_target_pairs={{0,1},{1,0},{2,3},{3,2},{4,5},{5,4},{6,7},{7,6},{8,9},{9,8},{10,11... | collective-permute-start | bytes 104 | tf_op jit(solution)/shard_map/ppermute | solution.py:18
  11.3 11.4 %collective-permute-start = (s32[8,16]{1,0:T(8,128)}, s32[8,16]{1,0:T(8,128)S(1)}, u32[]{:S(2)}, u32[]{:S(2)}) collective-permute-start(s32[8,16]{1,0:T(8,128)} %bitcast.169), channel_id=1, source_target_pairs={{0,1},{1,0},{2,3},{3,2},{4,5},{5,4},{6,7},{7,6},{8,9},{9,8},{10,11... | collective-permute-start | bytes 1544 | tf_op jit(solution)/shard_map/ppermute | solution.py:18
  12.5 45.8 %copy-start.2 = (bf16[1,384,512]{2,1,0:T(8,128)(2,1)S(1)}, bf16[1,384,512]{2,1,0:T(8,128)(2,1)}, u32[]{:S(2)}) copy-start(bf16[1,384,512]{2,1,0:T(8,128)(2,1)} %param.12) | copy-start | bytes 1179652
  13.7 45.5 %copy-start.3 = (bf16[1,384,512]{2,1,0:T(8,128)(2,1)S(1)}, bf16[1,384,512]{2,1,0:T(8,128)(2,1)}, u32[]{:S(2)}) copy-start(bf16[1,384,512]{2,1,0:T(8,128)(2,1)} %param.13) | copy-start | bytes 1179652
  13.7 46.3 %copy-start.9 = (bf16[1,8,4,4096]{3,2,1,0:T(4,128)(2,1)S(1)}, bf16[1,8,4,4096]{3,2,1,0:T(4,128)(2,1)}, u32[]{:S(2)}) copy-start(bf16[1,8,4,4096]{3,2,1,0:T(4,128)(2,1)} %param.14) | copy-start | bytes 786436
  50.5 32.4 %all-to-all-start.3 = ((bf16[8,8,8,4,256]{4,2,3,1,0:T(8,128)(2,1)}), bf16[8,8,8,4,256]{4,2,3,1,0:T(8,128)(2,1)}, u32[]{:S(2)}, u32[]{:S(2)}) async-start(bf16[8,8,8,4,256]{4,2,3,1,0:T(8,128)(2,1)} %bitcast.32), calls=%async_computation.3 | async-start | bytes 2097152 | tf_op jit(solution)/shard_map/all_to_all | solution.py:218
  57.5 161.2 %all-gather.10.cloned.1.call-start = ((), (), s32[]{:S(2)}) async-start(), calls=%async_computation.6 | async-start | bytes 3538944 | tf_op jit(solution)/shard_map/all_gather | solution.py:173
  61.0 6.3 %copy-start.15 = (bf16[1,8,4,512]{3,2,1,0:T(4,128)(2,1)S(1)}, bf16[1,8,4,512]{3,2,1,0:T(4,128)(2,1)}, u32[]{:S(2)}) copy-start(bf16[1,8,4,512]{3,2,1,0:T(4,128)(2,1)} %param.15) | copy-start | bytes 98308
  67.3 34.7 %copy-start.4 = (bf16[384,4,128]{2,1,0:T(4,128)(2,1)S(1)}, bf16[384,4,128]{2,1,0:T(4,128)(2,1)}, u32[]{:S(2)}) copy-start(bf16[384,4,128]{2,1,0:T(4,128)(2,1)} %reshape_squeeze.21) | copy-start | bytes 1179652
  67.3 92.9 %copy-start.13 = (pred[4,4]{1,0:T(4,128)(4,1)}, pred[4,4]{1,0:T(4,128)(4,1)S(1)}, u32[]{:S(2)}) copy-start(pred[4,4]{1,0:T(4,128)(4,1)S(1)} %iota_compare_fusion) | copy-start | bytes 52
  84.3 13.1 %collective-permute-start.6 = (bf16[8,8,4,256]{3,1,2,0:T(8,128)(2,1)S(1)}, bf16[8,8,4,256]{3,1,2,0:T(8,128)(2,1)S(1)}, u32[]{:S(2)}, u32[]{:S(2)}) collective-permute-start(bf16[8,8,4,256]{3,1,2,0:T(8,128)(2,1)S(1)} %reduce_sum.61), channel_id=1, source_target_pairs={{0,1},{1,0},{2,3},{3,2},{4,5},{5,4},{6,7},{7,6},{8,9},{9,8},{10,11... | collective-permute-start | bytes 393224 | tf_op jit(solution)/shard_map/ppermute | solution.py:18
  112.9 27.6 %all-to-all-start.1 = ((bf16[8,2,512]{2,1,0:T(2,128)(2,1)}), bf16[8,2,512]{2,1,0:T(2,128)(2,1)S(1)}, u32[]{:S(2)}, u32[]{:S(2)}) async-start(bf16[8,2,512]{2,1,0:T(2,128)(2,1)} %reshape.171), calls=%async_computation.1 | async-start | bytes 32768 | tf_op jit(solution)/shard_map/all_to_all | solution.py:209
  126.0 7.0 %copy-start.1 = (bf16[384,4,128]{2,1,0:T(4,128)(2,1)S(1)}, bf16[384,4,128]{2,1,0:T(4,128)(2,1)}, u32[]{:S(2)}) copy-start(bf16[384,4,128]{2,1,0:T(4,128)(2,1)} %reshape_squeeze.22) | copy-start | bytes 1179652
  137.5 22.5 %copy-start.6 = (f32[8,4,4,8]{0,3,1,2:T(8,128)S(1)}, f32[8,4,4,8]{0,3,1,2:T(8,128)}, u32[]{:S(2)}) copy-start(f32[8,4,4,8]{0,3,1,2:T(8,128)} %copy.155) | copy-start | bytes 12292
  137.5 23.3 %copy-start.7 = (f32[8,4,4,8,4]{3,4,1,2,0:T(4,128)S(1)}, f32[8,4,4,8,4]{3,4,1,2,0:T(4,128)}, u32[]{:S(2)}) copy-start(f32[8,4,4,8,4]{3,4,1,2,0:T(4,128)} %get-tuple-element.183) | copy-start | bytes 49156
  140.5 7.9 %all-to-all-start.2 = ((bf16[8,2,512]{2,1,0:T(2,128)(2,1)}), bf16[8,2,512]{2,1,0:T(2,128)(2,1)S(1)}, u32[]{:S(2)}, u32[]{:S(2)}) async-start(bf16[8,2,512]{2,1,0:T(2,128)(2,1)} %reshape.173), calls=%async_computation.2 | async-start | bytes 32768 | tf_op jit(solution)/shard_map/all_to_all | solution.py:212
  146.4 13.7 %collective-permute-start.4 = (bf16[8,4,4,8]{0,3,1,2:T(8,128)(2,1)S(1)}, bf16[8,4,4,8]{0,3,1,2:T(8,128)(2,1)S(1)}, u32[]{:S(2)}, u32[]{:S(2)}) collective-permute-start(bf16[8,4,4,8]{0,3,1,2:T(8,128)(2,1)S(1)} %bitcast_reduce_fusion), channel_id=1, source_target_pairs={{0,1},{1,0},{2,3},{3,2},{4,5},{5,4},{6,7},{7,6},{8,9},{9,8},{10,11... | collective-permute-start | bytes 6152 | tf_op jit(solution)/shard_map/ppermute | solution.py:18
  148.4 285.3 %all-to-all-start = ((bf16[8,8,4,4,8,128]{5,4,2,1,3,0:T(8,128)(2,1)}), bf16[8,8,4,4,8,128]{5,4,2,1,3,0:T(8,128)(2,1)}, u32[]{:S(2)}, u32[]{:S(2)}) async-start(bf16[8,8,4,4,8,128]{5,4,2,1,3,0:T(8,128)(2,1)} %copy.146), calls=%async_computation | async-start | bytes 4194304 | tf_op jit(solution)/shard_map/all_to_all | solution.py:215
  157.6 3.6 collective-permute-start.5
  160.2 0.6 copy-start.11
  218.7 215.0 %copy-start.5 = (f32[8,8,4,4,8]{4,2,1,3,0:T(4,128)S(1)}, f32[8,8,4,4,8]{4,2,1,3,0:T(4,128)}, u32[]{:S(2)}) copy-start(f32[8,8,4,4,8]{4,2,1,3,0:T(4,128)} %copy.150) | copy-start | bytes 98308
  437.0 6.9 %collective-permute-start.3 = (bf16[8,4,4,8,128]{4,3,1,2,0:T(8,128)(2,1)}, bf16[8,4,4,8,128]{4,3,1,2,0:T(8,128)(2,1)}, u32[]{:S(2)}, u32[]{:S(2)}) collective-permute-start(bf16[8,4,4,8,128]{4,3,1,2,0:T(8,128)(2,1)} %copy.221), channel_id=1, source_target_pairs={{0,1},{1,0},{2,3},{3,2},{4,5},{5,4},{6,7},{7,6},{8,9},{9,8},{10,11... | collective-permute-start | bytes 786440 | tf_op jit(solution)/shard_map/ppermute | solution.py:18
  437.4 6.5 %copy-start.8 = (f32[8,4,4,8,4]{3,4,1,2,0:T(4,128)S(1)}, f32[8,4,4,8,4]{3,4,1,2,0:T(4,128)}, u32[]{:S(2)}) copy-start(f32[8,4,4,8,4]{3,4,1,2,0:T(4,128)} %get-tuple-element.183) | copy-start | bytes 49156
  437.4 6.5 %copy-start.14 = (pred[4,4]{1,0:T(4,128)(4,1)S(1)}, pred[4,4]{1,0:T(4,128)(4,1)}, u32[]{:S(2)}) copy-start(pred[4,4]{1,0:T(4,128)(4,1)} %copy-done.13) | copy-start | bytes 52
  441.0 2.9 copy-start.12
Sparse Core Ops, SparseCore 0:
  10.7 48.1 all-gather.5
  61.1 67.3 all-gather.7
  130.7 88.0 all-gather.9
where the time goes:
time: 462 us; the launch traced here: 453 us
  matrix products  156 us (34%)
  other arithmetic  90 us (19%)
  waiting for transfers between devices  72.3 us (16%)
  local copies, waits for them, and re-layouts  44.6 us (10%)
  starting transfers between devices  43.6 us (9%)
  blocking collectives  30.9 us (7%)
  between operations  14.8 us (3%)
    dot_general x3, matrix products, fold_block(): jnp.einsum('kgrc,ckd->rkgd', weights.astype(jnp.bfloat16), value_heads, p...  73.6 us
    reduce_sum x3, other arithmetic, fold_block(): totals = totals * fading + jnp.sum(weights, axis=-1)  65.8 us
    dot_general x3, matrix products, fold_block(): jnp.einsum('rkgd,ckd->kgrc', query_heads, key_heads, preferred_element_ty...  60.3 us
    all_gather x1, waiting for transfers between devices, shards(): lax.all_gather(value_rows, 'seq', axis=0, tiled=True)  56.1 us
    all_gather x1, blocking collectives, shards(): lax.all_gather(sent_table, 'seq', axis=0, tiled=True)  25 us
    ppermute x7, starting transfers between devices, partner(): lax.ppermute(shard, axis, [(i, i ^ 1 << apart) for i in range(lax.axis_si...  17.8 us
    dynamic_slice x12, local copies, waits for them, and re-layouts, attend_piece(): lax.scan(advance, folded, (key_blocks, value_blocks, column_blocks))  14.1 us
    unnamed x43, local copies, waits for them, and re-layouts  12.4 us
  transfers between devices with their start and end apart: 14, of which 5 were waited for; matrix products, arithmetic and copies ran while one was open for 63% of the time, Pallas kernels for 0%

commit v1 on v0

v1 whole, which is shorter than its diff:
```python
import functools
import math

import jax
import jax.numpy as jnp
from jax import lax
from jax.experimental import pallas as pl
from jax.experimental.pallas import tpu as pltpu
from jax.sharding import PartitionSpec as P

HQ = 64
KVH = 8
HD = 128
PAGE = 128
GROUPS = HQ // KVH

neg_large = -1e30
SCALE2 = math.log2(math.e) / math.sqrt(HD)
NT = (((1,), (1,)), ((), ()))


def partner(shard, axis):
    return lax.ppermute(shard, axis, [(i, i ^ 1) for i in range(lax.axis_size(axis))])


def fold(q_ref, keys, values_t, g, mask, max_ref, total_ref, sum_ref, first):
    scores = lax.dot_general(
        keys, q_ref[:, g * HD : (g + 1) * HD], NT, preferred_element_type=jnp.float32
    ) * SCALE2
    if mask is not None:
        scores = jnp.where(mask, scores, neg_large)
    highest = jnp.max(scores, axis=0, keepdims=True)
    if not first:
        old_max = max_ref[g]
        highest = jnp.maximum(highest, old_max)
    weights = jnp.exp2(scores - highest)
    totals = jnp.sum(weights, axis=0, keepdims=True)
    update = jnp.dot(values_t, weights.astype(jnp.bfloat16), preferred_element_type=jnp.float32)
    if not first:
        fading = jnp.exp2(old_max - highest)
        totals = totals + total_ref[g] * fading
        update = update + sum_ref[g] * fading
    max_ref[g] = highest
    total_ref[g] = totals
    sum_ref[g] = update


def head_kernel(
    steps,
    members,
    owners_ref,
    q_ref,
    *refs,
):
    piece_refs = refs[:members]
    dq_ref, fresh_ref, counts_ref, checks_ref, out_ref, dout_ref, digest_ref = refs[members:-4]
    max_ref, total_ref, sum_ref, kv_ref = refs[-4:]
    rows = q_ref.shape[0]
    for c in range(members):
        kv_ref[c * rows : (c + 1) * rows] = piece_refs[c][...]
    row = lax.broadcasted_iota(jnp.int32, (rows, rows), 0)
    col = lax.broadcasted_iota(jnp.int32, (rows, rows), 1)
    own = kv_ref[:rows]
    own_t = own[:, HD:].T
    for g in range(GROUPS):
        fold(q_ref, own[:, :HD], own_t, g, row <= col, max_ref, total_ref, sum_ref, True)

    def advance(c, carry):
        @pl.when(owners_ref[c] < owners_ref[0])
        def _():
            kv = kv_ref[pl.ds(pl.multiple_of(c * rows, rows), rows)]
            kv_t = kv[:, HD:].T
            for g in range(GROUPS):
                fold(q_ref, kv[:, :HD], kv_t, g, None, max_ref, total_ref, sum_ref, False)

        return carry

    lax.fori_loop(1, members, advance, 0)
    for g in range(GROUPS):
        out_ref[:, g * HD : (g + 1) * HD] = (sum_ref[g] / total_ref[g]).T.astype(jnp.bfloat16)

    requests, tokens = counts_ref.shape
    asked = dq_ref.shape[0]
    per = asked // requests
    dq = dq_ref[...]
    counts = jnp.broadcast_to(counts_ref[...][:, None, :], (requests, per, tokens)).reshape(
        asked, tokens
    )
    scores = lax.dot_general(dq, kv_ref[:, :HD], NT, preferred_element_type=jnp.float32) * SCALE2
    live = counts > 0
    scores = jnp.where(live, scores, neg_large)
    fresh = fresh_ref[...]
    count_fresh = fresh.shape[0]
    fresh_scores = lax.dot_general(
        dq, fresh[:, :HD], NT, preferred_element_type=jnp.float32
    ) * SCALE2
    drow = lax.broadcasted_iota(jnp.int32, (asked, count_fresh), 0)
    dcol = lax.broadcasted_iota(jnp.int32, (asked, count_fresh), 1)
    allowed = (drow // per == dcol // steps) & (dcol % steps <= (drow % per) // GROUPS)
    fresh_scores = jnp.where(allowed, fresh_scores, neg_large)
    highest = jnp.maximum(
        jnp.max(scores, axis=1, keepdims=True), jnp.max(fresh_scores, axis=1, keepdims=True)
    )
    weights = jnp.exp2(scores - highest)
    fresh_weights = jnp.exp2(fresh_scores - highest)
    totals = jnp.sum(weights * counts, axis=1, keepdims=True) + jnp.sum(
        fresh_weights, axis=1, keepdims=True
    )
    weighted = (weights.astype(jnp.bfloat16).astype(jnp.float32) * counts).astype(jnp.bfloat16)
    summed = jnp.dot(weighted, kv_ref[:, HD:], preferred_element_type=jnp.float32)
    summed = summed + jnp.dot(
        fresh_weights.astype(jnp.bfloat16), fresh[:, HD:], preferred_element_type=jnp.float32
    )
    dout_ref[...] = (summed / totals).astype(jnp.bfloat16)
    both = jnp.dot(checks_ref[...], kv_ref[...], preferred_element_type=jnp.float32)
    half = both.shape[0] // 2
    digest_ref[...] = both[:half] + both[half:]


def one_head(head, steps, owners, query, pieces, dq, fresh, counts, checks):
    rows = query.shape[0]
    members = len(pieces)
    tokens = members * rows
    asked = dq.shape[1]
    whole = lambda a: pl.BlockSpec(a.shape, lambda i: (0,) * a.ndim)
    return pl.pallas_call(
        functools.partial(head_kernel, steps, members),
        grid=(1,),
        in_specs=[
            pl.BlockSpec(memory_space=pltpu.SMEM),
            pl.BlockSpec((rows, GROUPS * HD), lambda i: (0, head)),
            *[whole(piece) for piece in pieces],
            pl.BlockSpec((None, asked, HD), lambda i: (head, 0, 0)),
            pl.BlockSpec((None,) + fresh.shape[1:], lambda i: (head, 0, 0)),
            whole(counts),
            whole(checks),
        ],
        out_specs=[
            pl.BlockSpec((rows, GROUPS * HD), lambda i: (0, 0)),
            pl.BlockSpec((asked, HD), lambda i: (0, 0)),
            pl.BlockSpec((checks.shape[0] // 2, 2 * HD), lambda i: (0, 0)),
        ],
        out_shape=[
            jax.ShapeDtypeStruct((rows, GROUPS * HD), jnp.bfloat16),
            jax.ShapeDtypeStruct((asked, HD), jnp.bfloat16),
            jax.ShapeDtypeStruct((checks.shape[0] // 2, 2 * HD), jnp.float32),
        ],
        scratch_shapes=[
            pltpu.VMEM((GROUPS, 1, rows), jnp.float32),
            pltpu.VMEM((GROUPS, 1, rows), jnp.float32),
            pltpu.VMEM((GROUPS, HD, rows), jnp.float32),
            pltpu.VMEM((tokens, 2 * HD), jnp.bfloat16),
        ],
        compiler_params=pltpu.CompilerParams(vmem_limit_bytes=44 * 1024 * 1024),
        cost_estimate=pl.CostEstimate(
            flops=4 * rows * tokens * HD * GROUPS * 3,
            bytes_accessed=4 * rows * GROUPS * HD + 4 * tokens * HD,
            transcendentals=rows * tokens * GROUPS,
        ),
    )(owners, query, *pieces, dq, fresh, counts, checks)


def shards(
    prefill_query,
    prefill_keys,
    prefill_values,
    decode_query,
    decode_keys,
    decode_values,
    page_table,
    context_lengths,
    check_rows,
):
    key_rows = prefill_keys[0]
    value_rows = prefill_values[0]
    row_count = key_rows.shape[0]
    kv_local = key_rows.shape[1] // HD
    members = lax.axis_size("seq")
    me = lax.axis_index("seq")
    requests, step_count = decode_query.shape[1:3]
    asked = requests * step_count * GROUPS

    shifts = list(range(0, members, 2))
    line = [(me - s) % members for s in shifts]
    owners = jnp.stack(line + [((me ^ 1) - s) % members for s in shifts]).astype(jnp.int32)

    dq, dk, dv, table, lengths = partner(
        (decode_query[0], decode_keys[0], decode_values[0], page_table[0], context_lengths[0]),
        "grp",
    )
    dq = dq.reshape(requests, step_count, kv_local, GROUPS, HD)
    dq = jnp.transpose(dq, (2, 0, 1, 3, 4)).reshape(kv_local, asked, HD)
    fresh = jnp.concatenate(
        [a.reshape(requests * step_count, kv_local, HD) for a in (dk, dv)], axis=-1
    )
    fresh = jnp.transpose(fresh, (1, 0, 2))
    own_pages = row_count // PAGE
    max_pages = table.shape[1]
    page_ids = (owners[:, None] * own_pages + jnp.arange(own_pages, dtype=jnp.int32)).reshape(-1)
    hits = (table[:, :, None] == page_ids[None, None, :]).astype(jnp.float32)
    place = jnp.arange(max_pages * PAGE, dtype=jnp.int32).reshape(max_pages, PAGE)
    fits = (place[None] < lengths[:, None, None]).astype(jnp.float32)
    counts = jnp.einsum("ajp,ajo->apo", hits, fits)
    checks = counts[:, None] * check_rows.astype(jnp.float32)[None, :, None, :]
    counts = counts.reshape(requests, -1)
    check_count = check_rows.shape[0]
    checks = checks.reshape(requests * check_count, -1)
    upper = checks.astype(jnp.bfloat16)
    lower = (checks - upper.astype(jnp.float32)).astype(jnp.bfloat16)
    checks = jnp.concatenate([upper, lower], axis=0)

    pieces = []
    for h in range(kv_local):
        cut = slice(h * HD, (h + 1) * HD)
        own = jnp.concatenate([key_rows[:, cut], value_rows[:, cut]], axis=1)
        if h >= 2:
            pieces[h - 2], own = lax.optimization_barrier((pieces[h - 2], own))
        got = [own] + [
            lax.ppermute(own, "seq", [(i, (i + s) % members) for i in range(members)])
            for s in shifts[1:]
        ]
        pieces.append(got + [partner(b, "seq") for b in got])

    outs, douts, digests = [], [], []
    for h in range(kv_local):
        if h >= 1:
            pieces[h], outs[h - 1] = lax.optimization_barrier((pieces[h], outs[h - 1]))
        out, dout, digest = one_head(
            h, step_count, owners, prefill_query[0], pieces[h], dq, fresh, counts, checks
        )
        outs.append(out)
        douts.append(dout)
        digests.append(digest)
    prefill_out = jnp.concatenate(outs, axis=1)[None]
    dout = jnp.stack(douts, axis=0).reshape(kv_local, requests, step_count, GROUPS * HD)
    digest = jnp.stack(digests, axis=0).reshape(kv_local, requests, check_count, 2 * HD)
    dout, digest = partner((dout, digest), "grp")
    decode_out = jnp.transpose(dout, (1, 2, 0, 3)).reshape(requests, step_count, -1)[None]
    page_digest = jnp.transpose(digest, (1, 2, 0, 3)).reshape(requests, check_count, -1)[None]
    return (prefill_out, decode_out, page_digest)


def solution(mesh):
    in_specs = (
        P("grp", "seq", "tp"),
        P("grp", "seq", "tp"),
        P("grp", "seq", "tp"),
        P("grp", "seq", None, "tp"),
        P("grp", "seq", None, "tp"),
        P("grp", "seq", None, "tp"),
        P("grp", "seq", None),
        P("grp", "seq"),
        P(),
    )
    out_specs = (P("grp", "seq", "tp"), P("grp", "seq", None, "tp"), P("grp", "seq", None, "tp"))
    return jax.shard_map(shards, mesh=mesh, in_specs=in_specs, out_specs=out_specs, check_vma=False)
```

time: 462 us -> 212 us (0.46); the launches traced: 453 us -> 211 us
  matrix products: 156 us -> 0.32 us
  Pallas kernels: 0 us -> 115 us
  other arithmetic: 90 us -> 3.97 us
  waiting for transfers between devices: 72.3 us -> 27.5 us
  blocking collectives: 30.9 us -> 0 us
  local copies, waits for them, and re-layouts: 44.6 us -> 24.8 us
  between operations: 14.8 us -> 1.09 us
  starting transfers between devices: 43.6 us -> 38.5 us
    dot_general x14 -> x1, matrix products: 156 us -> 0.32 us  [shards(): counts = jnp.einsum('ajp,ajo->apo', hits, fits)]
    pallas_call x0 -> x4, Pallas kernels: none -> 115 us  [one_head(): pl.pallas_call(functools.partial(head_kernel, steps, members), grid=(1,),...]
    reduce_sum x8 -> x0, other arithmetic: 76.3 us -> none  [the longest x3 65.8 us: fold_block(): totals = totals * fading + jnp.sum(weights, axis=-1)]
    all_gather x3 -> x0, waiting for transfers between devices: 56.1 us -> none  [the longest x1 56.1 us: shards(): lax.all_gather(value_rows, 'seq', axis=0, tiled=True)]
    all_to_all x4 -> x0, starting transfers between devices: 25.8 us -> none  [the longest x1 7.69 us: shards(): lax.all_to_all(by_owner[2].astype(jnp.bfloat16), 'seq', split_axis=0, con...]
    ppermute x7 -> x35, waiting for transfers between devices: 2.35 us -> 27.5 us  [the longest x12 15.5 us: shards(): lax.ppermute(own, 'seq', [(i, (i + s) % members) for i in range(members)])]
    all_gather x1 -> x0, blocking collectives: 25 us -> none  [shards(): lax.all_gather(sent_table, 'seq', axis=0, tiled=True)]
    ppermute x7 -> x35, starting transfers between devices: 17.8 us -> 38.5 us  [the longest x23 24.2 us: partner(): lax.ppermute(shard, axis, [(i, i ^ 1) for i in range(lax.axis_size(axis))])]
  transfers between devices with their start and end apart: 14 -> 35, of which waited for: 5 -> 8; matrix products, arithmetic and copies ran while one was open for 63% -> 5% of each run, Pallas kernels for 0% -> 41%
where the time goes in v1:
time: 212 us; the launch traced here: 211 us
  Pallas kernels  115 us (54%)
  starting transfers between devices  38.5 us (18%)
  waiting for transfers between devices  27.5 us (13%)
  local copies, waits for them, and re-layouts  24.8 us (12%)
  other arithmetic  3.97 us (2%)
    pallas_call x4, Pallas kernels, one_head(): pl.pallas_call(functools.partial(head_kernel, steps, members), grid=(1,),...  115 us
    ppermute x23, starting transfers between devices, partner(): lax.ppermute(shard, axis, [(i, i ^ 1) for i in range(lax.axis_size(axis))])  24.2 us
    ppermute x12, waiting for transfers between devices, shards(): lax.ppermute(own, 'seq', [(i, (i + s) % members) for i in range(members)])  15.5 us
    unnamed x73, local copies, waits for them, and re-layouts  14.7 us
    ppermute x12, starting transfers between devices, shards(): lax.ppermute(own, 'seq', [(i, (i + s) % members) for i in range(members)])  14.3 us
    ppermute x23, waiting for transfers between devices, partner(): lax.ppermute(shard, axis, [(i, i ^ 1) for i in range(lax.axis_size(axis))])  12 us
  transfers between devices with their start and end apart: 35, of which 8 were waited for; matrix products, arithmetic and copies ran while one was open for 5% of the time, Pallas kernels for 41%

profile of v1, /device:TPU:27, one launch (start us, length us, event | category | flops | bytes accessed | tf_op | source)
XLA Modules:
  0.0 211.0 jit_solution(15991460648942953708)
XLA Ops:
  0.7 1.1 fusion.8
  1.8 1.1 fusion.9
  3.0 1.3 collective-permute-start.8
  4.3 0.2 collective-permute-start.9
  4.5 1.5 collective-permute-start.17
  6.2 0.7 pad_maximum_fusion.4
  7.0 0.2 collective-permute-done.18
  7.3 0.4 collective-permute-start.15
  7.8 0.3 fusion.1
  8.1 0.4 collective-permute-done.15
  8.5 0.3 collective-permute-start.10
  8.8 3.1 %collective-permute-start = (bf16[384,256]{1,0:T(8,128)(2,1)S(1)}, bf16[384,256]{1,0:T(8,128)(2,1)S(1)}, u32[]{:S(2)}, u32[]{:S(2)}) collective-permute-start(bf16[384,256]{1,0:T(8,128)(2,1)S(1)} %pad_maximum_fusion.3.refs_0_), channel_id=1, source_target_pairs={{0,8},{4,12},{8,16},{12,20},{16,24},{20,28},{24,0},{28,4},{1,9},{5... | collective-permute-start | bytes 589832 | tf_op jit(solution)/shard_map/ppermute | solution.py:219
  12.1 9.3 %collective-permute-done.8.refs_2_ = bf16[384,256]{1,0:T(8,128)(2,1)S(1)} collective-permute-done((bf16[384,256]{1,0:T(8,128)(2,1)S(1)}, bf16[384,256]{1,0:T(8,128)(2,1)S(1)}, u32[]{:S(2)}, u32[]{:S(2)}) %collective-permute-start.8) | collective-permute-done | bytes 196640 | tf_op jit(solution)/shard_map/ppermute | solution.py:219
  21.4 9.0 %collective-permute-start.14 = (bf16[8,4,4096]{2,1,0:T(4,128)(2,1)S(1)}, bf16[8,4,4096]{2,1,0:T(4,128)(2,1)S(1)}, u32[]{:S(2)}, u32[]{:S(2)}) collective-permute-start(bf16[8,4,4096]{2,1,0:T(4,128)(2,1)S(1)} %bitcast.62), channel_id=1, source_target_pairs={{0,1},{1,0},{2,3},{3,2},{4,5},{5,4},{6,7},{7,6},{8,9},{9,8},{10,11... | collective-permute-start | bytes 786440 | tf_op jit(solution)/shard_map/ppermute | solution.py:23
  30.4 0.3 collective-permute-start.11
  30.7 1.2 collective-permute-start.12
  32.0 6.2 %collective-permute-done.1.refs_2_ = bf16[384,256]{1,0:T(8,128)(2,1)S(1)} collective-permute-done((bf16[384,256]{1,0:T(8,128)(2,1)S(1)}, bf16[384,256]{1,0:T(8,128)(2,1)S(1)}, u32[]{:S(2)}, u32[]{:S(2)}) %collective-permute-start.1) | collective-permute-done | bytes 196640 | tf_op jit(solution)/shard_map/ppermute | solution.py:219
  38.2 0.3 collective-permute-start.3
  38.4 1.2 collective-permute-start.13
  39.6 0.3 collective-permute-start.4
  39.9 0.7 copy-done.26
  40.6 1.2 collective-permute-start.5
  41.8 0.7 copy-done.28
  42.4 0.3 collective-permute-start.6
  42.9 1.0 reshape.137
  43.9 1.0 copy.15
  44.9 3.8 %collective-permute-done.13.refs_7_ = bf16[384,256]{1,0:T(8,128)(2,1)} collective-permute-done((bf16[384,256]{1,0:T(8,128)(2,1)S(1)}, bf16[384,256]{1,0:T(8,128)(2,1)}, u32[]{:S(2)}, u32[]{:S(2)}) %collective-permute-start.13) | collective-permute-done | bytes 196640 | tf_op jit(solution)/shard_map/ppermute | solution.py:23
  48.7 4.4 %collective-permute-start.19 = (bf16[384,256]{1,0:T(8,128)(2,1)S(1)}, bf16[384,256]{1,0:T(8,128)(2,1)}, u32[]{:S(2)}, u32[]{:S(2)}) collective-permute-start(bf16[384,256]{1,0:T(8,128)(2,1)S(1)} %get-tuple-element.90.refs_0_), channel_id=1, source_target_pairs={{0,8},{4,12},{8,16},{12,20},{16,24},{20,28},{24,0},{28,4},{1,9},{5... | collective-permute-start | bytes 589832 | tf_op jit(solution)/shard_map/ppermute | solution.py:219
  53.1 0.6 collective-permute-start.21
  53.6 3.5 %collective-permute-done.5.refs_6_ = bf16[384,256]{1,0:T(8,128)(2,1)} collective-permute-done((bf16[384,256]{1,0:T(8,128)(2,1)S(1)}, bf16[384,256]{1,0:T(8,128)(2,1)}, u32[]{:S(2)}, u32[]{:S(2)}) %collective-permute-start.5) | collective-permute-done | bytes 196640 | tf_op jit(solution)/shard_map/ppermute | solution.py:23
  57.1 0.3 collective-permute-start.22
  57.4 4.0 %collective-permute-done.6.refs_7_ = bf16[384,256]{1,0:T(8,128)(2,1)} collective-permute-done((bf16[384,256]{1,0:T(8,128)(2,1)S(1)}, bf16[384,256]{1,0:T(8,128)(2,1)}, u32[]{:S(2)}, u32[]{:S(2)}) %collective-permute-start.6) | collective-permute-done | bytes 196640 | tf_op jit(solution)/shard_map/ppermute | solution.py:23
  61.3 4.4 %collective-permute-start.26 = (bf16[384,256]{1,0:T(8,128)(2,1)}, bf16[384,256]{1,0:T(8,128)(2,1)S(1)}, u32[]{:S(2)}, u32[]{:S(2)}) collective-permute-start(bf16[384,256]{1,0:T(8,128)(2,1)} %get-tuple-element.100.refs_0_), channel_id=1, source_target_pairs={{0,8},{4,12},{8,16},{12,20},{16,24},{20,28},{24,0},{28,4},{1,9},{5... | collective-permute-start | bytes 589832 | tf_op jit(solution)/shard_map/ppermute | solution.py:219
  65.7 1.9 copy-done.12
  67.6 0.9 copy-done.21
  68.6 0.9 copy-done.27
  69.5 0.9 copy-done.29
  70.4 28.5 %shard_map.112 = (bf16[384,1024]{1,0:T(8,128)(2,1)S(1)}, bf16[256,128]{1,0:T(8,128)(2,1)S(1)}, f32[64,256]{1,0:T(8,128)S(1)}) custom-call(s32[8]{0:T(128)S(1)} %stack.65.owners_ref, bf16[384,4096]{1,0:T(8,128)(2,1)S(1)} %bitcast.53, bf16[384,256]{1,0:T(8,128)(2,1)S(1)} %pad_maximum_fusion.5.refs_0_, bf16[384,256]{1,0:T(8,128)(2,1)S(1)} %collective-permute-done.7.refs_1_, ...), custom_call_target="tpu_custom_call" | custom-call | flops 14495514624 | bytes 3145728 | tf_op jit(solution)/shard_map/pallas_call | solution.py:126
  99.0 0.6 copy-done.8
  99.6 0.2 collective-permute-start.28
  99.9 1.4 collective-permute-start.24
  101.5 28.7 %shard_map.113 = (bf16[384,1024]{1,0:T(8,128)(2,1)S(1)}, bf16[256,128]{1,0:T(8,128)(2,1)S(1)}, f32[64,256]{1,0:T(8,128)S(1)}) custom-call(s32[8]{0:T(128)S(1)} %stack.65.owners_ref, bf16[384,4096]{1,0:T(8,128)(2,1)S(1)} %bitcast.54, bf16[384,256]{1,0:T(8,128)(2,1)S(1)} %pad_maximum_fusion.3.refs_0_, bf16[384,256]{1,0:T(8,128)(2,1)S(1)} %copy-done.15, ...), custom_call_target="tpu_custom_call" | custom-call | flops 14495514624 | bytes 3145728 | tf_op jit(solution)/shard_map/pallas_call | solution.py:126
  130.2 0.6 stack.67
  130.8 0.6 stack.66
  131.5 1.5 collective-permute-start.30
  133.0 0.7 copy-done.30
  133.7 1.4 collective-permute-start.32
  135.1 0.9 copy-done.3
  136.1 0.8 copy-done.5
  136.9 1.9 copy-done.13
  138.8 0.9 copy-done.25
  139.7 0.9 copy-done.31
  140.6 29.0 %shard_map.114 = (bf16[384,1024]{1,0:T(8,128)(2,1)S(1)}, bf16[256,128]{1,0:T(8,128)(2,1)S(1)}, f32[64,256]{1,0:T(8,128)S(1)}) custom-call(s32[8]{0:T(128)S(1)} %stack.65.owners_ref, bf16[384,4096]{1,0:T(8,128)(2,1)S(1)} %bitcast.55, bf16[384,256]{1,0:T(8,128)(2,1)S(1)} %copy-done.3, bf16[384,256]{1,0:T(8,128)(2,1)} %collective-permute-done.19.refs_1_, ...), custom_call_target="tpu_custom_call" | custom-call | flops 14495514624 | bytes 3145728 | tf_op jit(solution)/shard_map/pallas_call | solution.py:126
  169.7 1.1 copy-done.1
  170.8 28.6 %shard_map.115 = (bf16[384,1024]{1,0:T(8,128)(2,1)S(1)}, bf16[256,128]{1,0:T(8,128)(2,1)S(1)}, f32[64,256]{1,0:T(8,128)S(1)}) custom-call(s32[8]{0:T(128)S(1)} %stack.65.owners_ref, bf16[384,4096]{1,0:T(8,128)(2,1)S(1)} %bitcast.56, bf16[384,256]{1,0:T(8,128)(2,1)} %get-tuple-element.100.refs_0_, bf16[384,256]{1,0:T(8,128)(2,1)S(1)} %copy-done.23, ...), custom_call_target="tpu_custom_call" | custom-call | flops 14495514624 | bytes 3145728 | tf_op jit(solution)/shard_map/pallas_call | solution.py:126
  199.5 0.6 copy-done.7
  200.2 3.3 %collective-permute-start.34 = (f32[4,8,8,256]{3,2,1,0:T(8,128)S(1)}, f32[4,8,8,256]{3,2,1,0:T(8,128)}, u32[]{:S(2)}, u32[]{:S(2)}) collective-permute-start(f32[4,8,8,256]{3,2,1,0:T(8,128)S(1)} %pad_maximum_fusion.2), channel_id=1, source_target_pairs={{0,1},{1,0},{2,3},{3,2},{4,5},{5,4},{6,7},{7,6},{8,9},{9,8},{10,11... | collective-permute-start | bytes 786440 | tf_op jit(solution)/shard_map/ppermute | solution.py:23
  203.5 0.9 stack.69
  204.4 0.9 stack.68
  205.2 1.1 pad_maximum_fusion.1
  206.4 1.8 maximum_bitcast_fusion
  208.2 1.7 copy.19
  209.9 0.2 copy.18
  210.1 0.9 broadcast_in_dim_reshape.17
  (115 shorter events, 1.5 us)
Async XLA Ops:
  0.6 6.4 %copy-start.32 = (bf16[8,128]{1,0:T(8,128)(2,1)S(1)}, bf16[8,128]{1,0:T(8,128)(2,1)}, u32[]{:S(2)}) copy-start(bf16[8,128]{1,0:T(8,128)(2,1)} %param.17) | copy-start | bytes 6148
  0.6 6.6 %copy-start.34 = (bf16[1,8,4,512]{3,2,1,0:T(4,128)(2,1)S(1)}, bf16[1,8,4,512]{3,2,1,0:T(4,128)(2,1)}, u32[]{:S(2)}) copy-start(bf16[1,8,4,512]{3,2,1,0:T(4,128)(2,1)} %param.13) | copy-start | bytes 98308
  0.7 7.0 %copy-start.35 = (bf16[1,8,4,512]{3,2,1,0:T(4,128)(2,1)S(1)}, bf16[1,8,4,512]{3,2,1,0:T(4,128)(2,1)}, u32[]{:S(2)}) copy-start(bf16[1,8,4,512]{3,2,1,0:T(4,128)(2,1)} %param.14) | copy-start | bytes 98308
  0.7 20.7 %copy-start.33 = (bf16[1,8,4,4096]{3,2,1,0:T(4,128)(2,1)S(1)}, bf16[1,8,4,4096]{3,2,1,0:T(4,128)(2,1)}, u32[]{:S(2)}) copy-start(bf16[1,8,4,4096]{3,2,1,0:T(4,128)(2,1)} %param.12) | copy-start | bytes 786436
  2.9 9.1 %collective-permute-start.7 = (bf16[384,256]{1,0:T(8,128)(2,1)S(1)}, bf16[384,256]{1,0:T(8,128)(2,1)S(1)}, u32[]{:S(2)}, u32[]{:S(2)}) collective-permute-start(bf16[384,256]{1,0:T(8,128)(2,1)S(1)} %pad_maximum_fusion.5.refs_0_), channel_id=1, source_target_pairs={{0,8},{4,12},{8,16},{12,20},{16,24},{20,28},{24,0},{28,4},{1,9},{5... | collective-permute-start | bytes 589832 | tf_op jit(solution)/shard_map/ppermute | solution.py:219
  3.0 18.4 %collective-permute-start.8 = (bf16[384,256]{1,0:T(8,128)(2,1)S(1)}, bf16[384,256]{1,0:T(8,128)(2,1)S(1)}, u32[]{:S(2)}, u32[]{:S(2)}) collective-permute-start(bf16[384,256]{1,0:T(8,128)(2,1)S(1)} %pad_maximum_fusion.5.refs_0_), channel_id=1, source_target_pairs={{0,16},{4,20},{8,24},{12,28},{16,0},{20,4},{24,8},{28,12},{1,17},{... | collective-permute-start | bytes 589832 | tf_op jit(solution)/shard_map/ppermute | solution.py:219
  4.3 17.1 %collective-permute-start.9 = (bf16[384,256]{1,0:T(8,128)(2,1)S(1)}, bf16[384,256]{1,0:T(8,128)(2,1)S(1)}, u32[]{:S(2)}, u32[]{:S(2)}) collective-permute-start(bf16[384,256]{1,0:T(8,128)(2,1)S(1)} %pad_maximum_fusion.5.refs_0_), channel_id=1, source_target_pairs={{0,24},{4,28},{8,0},{12,4},{16,8},{20,12},{24,16},{28,20},{1,25},{... | collective-permute-start | bytes 589832 | tf_op jit(solution)/shard_map/ppermute | solution.py:219
  4.5 3.1 %collective-permute-start.17 = (s32[8,16]{1,0:T(8,128)}, s32[8,16]{1,0:T(8,128)S(1)}, u32[]{:S(2)}, u32[]{:S(2)}) collective-permute-start(s32[8,16]{1,0:T(8,128)} %bitcast.65), channel_id=1, source_target_pairs={{0,1},{1,0},{2,3},{3,2},{4,5},{5,4},{6,7},{7,6},{8,9},{9,8},{10,11... | collective-permute-start | bytes 1544 | tf_op jit(solution)/shard_map/ppermute | solution.py:23
  6.0 1.3 collective-permute-start.18
  6.9 92.0 %copy-start.2 = (bf16[384,256]{1,0:T(8,128)(2,1)}, bf16[384,256]{1,0:T(8,128)(2,1)S(1)}, u32[]{:S(2)}) copy-start(bf16[384,256]{1,0:T(8,128)(2,1)S(1)} %get-tuple-element.90.refs_0_) | copy-start | bytes 589828
  7.3 1.2 collective-permute-start.15
  7.6 1.2 collective-permute-start.16
  8.5 21.9 %collective-permute-start.10 = (bf16[384,256]{1,0:T(8,128)(2,1)S(1)}, bf16[384,256]{1,0:T(8,128)(2,1)S(1)}, u32[]{:S(2)}, u32[]{:S(2)}) collective-permute-start(bf16[384,256]{1,0:T(8,128)(2,1)S(1)} %pad_maximum_fusion.5.refs_0_), channel_id=1, source_target_pairs={{0,4},{4,0},{8,12},{12,8},{16,20},{20,16},{24,28},{28,24},{1,5},{5... | collective-permute-start | bytes 589832 | tf_op jit(solution)/shard_map/ppermute | solution.py:23
  8.8 21.8 %collective-permute-start = (bf16[384,256]{1,0:T(8,128)(2,1)S(1)}, bf16[384,256]{1,0:T(8,128)(2,1)S(1)}, u32[]{:S(2)}, u32[]{:S(2)}) collective-permute-start(bf16[384,256]{1,0:T(8,128)(2,1)S(1)} %pad_maximum_fusion.3.refs_0_), channel_id=1, source_target_pairs={{0,8},{4,12},{8,16},{12,20},{16,24},{20,28},{24,0},{28,4},{1,9},{5... | collective-permute-start | bytes 589832 | tf_op jit(solution)/shard_map/ppermute | solution.py:219
  12.0 26.2 %collective-permute-start.1 = (bf16[384,256]{1,0:T(8,128)(2,1)S(1)}, bf16[384,256]{1,0:T(8,128)(2,1)S(1)}, u32[]{:S(2)}, u32[]{:S(2)}) collective-permute-start(bf16[384,256]{1,0:T(8,128)(2,1)S(1)} %pad_maximum_fusion.3.refs_0_), channel_id=1, source_target_pairs={{0,16},{4,20},{8,24},{12,28},{16,0},{20,4},{24,8},{28,12},{1,17},{... | collective-permute-start | bytes 589832 | tf_op jit(solution)/shard_map/ppermute | solution.py:219
  21.4 17.1 %collective-permute-start.2 = (bf16[384,256]{1,0:T(8,128)(2,1)S(1)}, bf16[384,256]{1,0:T(8,128)(2,1)S(1)}, u32[]{:S(2)}, u32[]{:S(2)}) collective-permute-start(bf16[384,256]{1,0:T(8,128)(2,1)S(1)} %pad_maximum_fusion.3.refs_0_), channel_id=1, source_target_pairs={{0,24},{4,28},{8,0},{12,4},{16,8},{20,12},{24,16},{28,20},{1,25},{... | collective-permute-start | bytes 589832 | tf_op jit(solution)/shard_map/ppermute | solution.py:219
  21.4 18.3 %collective-permute-start.14 = (bf16[8,4,4096]{2,1,0:T(4,128)(2,1)S(1)}, bf16[8,4,4096]{2,1,0:T(4,128)(2,1)S(1)}, u32[]{:S(2)}, u32[]{:S(2)}) collective-permute-start(bf16[8,4,4096]{2,1,0:T(4,128)(2,1)S(1)} %bitcast.62), channel_id=1, source_target_pairs={{0,1},{1,0},{2,3},{3,2},{4,5},{5,4},{6,7},{7,6},{8,9},{9,8},{10,11... | collective-permute-start | bytes 786440 | tf_op jit(solution)/shard_map/ppermute | solution.py:23
  30.4 35.3 %copy-start.20 = (bf16[384,256]{1,0:T(8,128)(2,1)}, bf16[384,256]{1,0:T(8,128)(2,1)S(1)}, u32[]{:S(2)}) copy-start(bf16[384,256]{1,0:T(8,128)(2,1)S(1)} %collective-permute-done.10.refs_4_) | copy-start | bytes 589828
  30.4 9.5 %collective-permute-start.11 = (bf16[384,256]{1,0:T(8,128)(2,1)S(1)}, bf16[384,256]{1,0:T(8,128)(2,1)S(1)}, u32[]{:S(2)}, u32[]{:S(2)}) collective-permute-start(bf16[384,256]{1,0:T(8,128)(2,1)S(1)} %collective-permute-done.7.refs_1_), channel_id=1, source_target_pairs={{0,4},{4,0},{8,12},{12,8},{16,20},{20,16},{24,28},{28,24},{1,5},{5... | collective-permute-start | bytes 589832 | tf_op jit(solution)/shard_map/ppermute | solution.py:23
  30.7 35.1 %copy-start.14 = (bf16[384,256]{1,0:T(8,128)(2,1)}, bf16[384,256]{1,0:T(8,128)(2,1)S(1)}, u32[]{:S(2)}) copy-start(bf16[384,256]{1,0:T(8,128)(2,1)S(1)} %collective-permute-done.refs_1_) | copy-start | bytes 589828
  30.7 11.1 %collective-permute-start.12 = (bf16[384,256]{1,0:T(8,128)(2,1)S(1)}, bf16[384,256]{1,0:T(8,128)(2,1)S(1)}, u32[]{:S(2)}, u32[]{:S(2)}) collective-permute-start(bf16[384,256]{1,0:T(8,128)(2,1)S(1)} %collective-permute-done.8.refs_2_), channel_id=1, source_target_pairs={{0,4},{4,0},{8,12},{12,8},{16,20},{20,16},{24,28},{28,24},{1,5},{5... | collective-permute-start | bytes 589832 | tf_op jit(solution)/shard_map/ppermute | solution.py:23
  38.2 27.6 %copy-start.16 = (bf16[384,256]{1,0:T(8,128)(2,1)}, bf16[384,256]{1,0:T(8,128)(2,1)S(1)}, u32[]{:S(2)}) copy-start(bf16[384,256]{1,0:T(8,128)(2,1)S(1)} %collective-permute-done.1.refs_2_) | copy-start | bytes 589828
  38.2 14.9 %collective-permute-start.3 = (bf16[384,256]{1,0:T(8,128)(2,1)S(1)}, bf16[384,256]{1,0:T(8,128)(2,1)}, u32[]{:S(2)}, u32[]{:S(2)}) collective-permute-start(bf16[384,256]{1,0:T(8,128)(2,1)S(1)} %pad_maximum_fusion.3.refs_0_), channel_id=1, source_target_pairs={{0,4},{4,0},{8,12},{12,8},{16,20},{20,16},{24,28},{28,24},{1,5},{5... | collective-permute-start | bytes 589832 | tf_op jit(solution)/shard_map/ppermute | solution.py:23
  38.4 27.3 %copy-start.18 = (bf16[384,256]{1,0:T(8,128)(2,1)}, bf16[384,256]{1,0:T(8,128)(2,1)S(1)}, u32[]{:S(2)}) copy-start(bf16[384,256]{1,0:T(8,128)(2,1)S(1)} %collective-permute-done.2.refs_3_) | copy-start | bytes 589828
  38.4 10.3 %collective-permute-start.13 = (bf16[384,256]{1,0:T(8,128)(2,1)S(1)}, bf16[384,256]{1,0:T(8,128)(2,1)}, u32[]{:S(2)}, u32[]{:S(2)}) collective-permute-start(bf16[384,256]{1,0:T(8,128)(2,1)S(1)} %collective-permute-done.9.refs_3_), channel_id=1, source_target_pairs={{0,4},{4,0},{8,12},{12,8},{16,20},{20,16},{24,28},{28,24},{1,5},{5... | collective-permute-start | bytes 589832 | tf_op jit(solution)/shard_map/ppermute | solution.py:23
  39.6 13.5 %collective-permute-start.4 = (bf16[384,256]{1,0:T(8,128)(2,1)S(1)}, bf16[384,256]{1,0:T(8,128)(2,1)}, u32[]{:S(2)}, u32[]{:S(2)}) collective-permute-start(bf16[384,256]{1,0:T(8,128)(2,1)S(1)} %collective-permute-done.refs_1_), channel_id=1, source_target_pairs={{0,4},{4,0},{8,12},{12,8},{16,20},{20,16},{24,28},{28,24},{1,5},{5... | collective-permute-start | bytes 589832 | tf_op jit(solution)/shard_map/ppermute | solution.py:23
  40.6 16.6 %collective-permute-start.5 = (bf16[384,256]{1,0:T(8,128)(2,1)S(1)}, bf16[384,256]{1,0:T(8,128)(2,1)}, u32[]{:S(2)}, u32[]{:S(2)}) collective-permute-start(bf16[384,256]{1,0:T(8,128)(2,1)S(1)} %collective-permute-done.1.refs_2_), channel_id=1, source_target_pairs={{0,4},{4,0},{8,12},{12,8},{16,20},{20,16},{24,28},{28,24},{1,5},{5... | collective-permute-start | bytes 589832 | tf_op jit(solution)/shard_map/ppermute | solution.py:23
  42.4 18.9 %collective-permute-start.6 = (bf16[384,256]{1,0:T(8,128)(2,1)S(1)}, bf16[384,256]{1,0:T(8,128)(2,1)}, u32[]{:S(2)}, u32[]{:S(2)}) collective-permute-start(bf16[384,256]{1,0:T(8,128)(2,1)S(1)} %collective-permute-done.2.refs_3_), channel_id=1, source_target_pairs={{0,4},{4,0},{8,12},{12,8},{16,20},{20,16},{24,28},{28,24},{1,5},{5... | collective-permute-start | bytes 589832 | tf_op jit(solution)/shard_map/ppermute | solution.py:23
  42.8 92.4 %copy-start = (bf16[128,3072]{1,0:T(8,128)(2,1)}, bf16[128,3072]{1,0:T(8,128)(2,1)S(1)}, u32[]{:S(2)}) copy-start(bf16[128,3072]{1,0:T(8,128)(2,1)S(1)} %pad_maximum_fusion.refs_11_) | copy-start | bytes 2359300
  42.9 58.6 %copy-start.4 = (bf16[4,32,256]{2,1,0:T(8,128)(2,1)}, bf16[4,32,256]{2,1,0:T(8,128)(2,1)S(1)}, u32[]{:S(2)}) copy-start(bf16[4,32,256]{2,1,0:T(8,128)(2,1)S(1)} %maximum_bitcast_fusion.1.refs_9_) | copy-start | bytes 196612
  48.7 50.9 %collective-permute-start.19 = (bf16[384,256]{1,0:T(8,128)(2,1)S(1)}, bf16[384,256]{1,0:T(8,128)(2,1)}, u32[]{:S(2)}, u32[]{:S(2)}) collective-permute-start(bf16[384,256]{1,0:T(8,128)(2,1)S(1)} %get-tuple-element.90.refs_0_), channel_id=1, source_target_pairs={{0,8},{4,12},{8,16},{12,20},{16,24},{20,28},{24,0},{28,4},{1,9},{5... | collective-permute-start | bytes 589832 | tf_op jit(solution)/shard_map/ppermute | solution.py:219
  53.1 46.5 %collective-permute-start.20 = (bf16[384,256]{1,0:T(8,128)(2,1)S(1)}, bf16[384,256]{1,0:T(8,128)(2,1)}, u32[]{:S(2)}, u32[]{:S(2)}) collective-permute-start(bf16[384,256]{1,0:T(8,128)(2,1)S(1)} %get-tuple-element.90.refs_0_), channel_id=1, source_target_pairs={{0,16},{4,20},{8,24},{12,28},{16,0},{20,4},{24,8},{28,12},{1,17},{... | collective-permute-start | bytes 589832 | tf_op jit(solution)/shard_map/ppermute | solution.py:219
  53.1 46.7 %collective-permute-start.21 = (bf16[384,256]{1,0:T(8,128)(2,1)S(1)}, bf16[384,256]{1,0:T(8,128)(2,1)}, u32[]{:S(2)}, u32[]{:S(2)}) collective-permute-start(bf16[384,256]{1,0:T(8,128)(2,1)S(1)} %get-tuple-element.90.refs_0_), channel_id=1, source_target_pairs={{0,24},{4,28},{8,0},{12,4},{16,8},{20,12},{24,16},{28,20},{1,25},{... | collective-permute-start | bytes 589832 | tf_op jit(solution)/shard_map/ppermute | solution.py:219
  57.1 42.8 %collective-permute-start.22 = (bf16[384,256]{1,0:T(8,128)(2,1)S(1)}, bf16[384,256]{1,0:T(8,128)(2,1)S(1)}, u32[]{:S(2)}, u32[]{:S(2)}) collective-permute-start(bf16[384,256]{1,0:T(8,128)(2,1)S(1)} %get-tuple-element.90.refs_0_), channel_id=1, source_target_pairs={{0,4},{4,0},{8,12},{12,8},{16,20},{20,16},{24,28},{28,24},{1,5},{5... | collective-permute-start | bytes 589832 | tf_op jit(solution)/shard_map/ppermute | solution.py:23
  61.3 40.0 %collective-permute-start.26 = (bf16[384,256]{1,0:T(8,128)(2,1)}, bf16[384,256]{1,0:T(8,128)(2,1)S(1)}, u32[]{:S(2)}, u32[]{:S(2)}) collective-permute-start(bf16[384,256]{1,0:T(8,128)(2,1)} %get-tuple-element.100.refs_0_), channel_id=1, source_target_pairs={{0,8},{4,12},{8,16},{12,20},{16,24},{20,28},{24,0},{28,4},{1,9},{5... | collective-permute-start | bytes 589832 | tf_op jit(solution)/shard_map/ppermute | solution.py:219
  65.7 1.9 copy-start.12
  67.6 0.9 copy-start.21
  68.6 0.9 copy-start.27
  69.5 0.9 copy-start.29
  70.4 31.1 %copy-start.15 = (bf16[384,256]{1,0:T(8,128)(2,1)S(1)}, bf16[384,256]{1,0:T(8,128)(2,1)}, u32[]{:S(2)}) copy-start(bf16[384,256]{1,0:T(8,128)(2,1)} %copy-done.14) | copy-start | bytes 589828
  70.4 31.1 %copy-start.17 = (bf16[384,256]{1,0:T(8,128)(2,1)S(1)}, bf16[384,256]{1,0:T(8,128)(2,1)}, u32[]{:S(2)}) copy-start(bf16[384,256]{1,0:T(8,128)(2,1)} %copy-done.16) | copy-start | bytes 589828
  70.4 31.1 %copy-start.19 = (bf16[384,256]{1,0:T(8,128)(2,1)S(1)}, bf16[384,256]{1,0:T(8,128)(2,1)}, u32[]{:S(2)}) copy-start(bf16[384,256]{1,0:T(8,128)(2,1)} %copy-done.18) | copy-start | bytes 589828
  99.6 31.9 %collective-permute-start.27 = (bf16[384,256]{1,0:T(8,128)(2,1)}, bf16[384,256]{1,0:T(8,128)(2,1)}, u32[]{:S(2)}, u32[]{:S(2)}) collective-permute-start(bf16[384,256]{1,0:T(8,128)(2,1)} %get-tuple-element.100.refs_0_), channel_id=1, source_target_pairs={{0,16},{4,20},{8,24},{12,28},{16,0},{20,4},{24,8},{28,12},{1,17},{... | collective-permute-start | bytes 589832 | tf_op jit(solution)/shard_map/ppermute | solution.py:219
  99.6 31.9 %collective-permute-start.28 = (bf16[384,256]{1,0:T(8,128)(2,1)}, bf16[384,256]{1,0:T(8,128)(2,1)}, u32[]{:S(2)}, u32[]{:S(2)}) collective-permute-start(bf16[384,256]{1,0:T(8,128)(2,1)} %get-tuple-element.100.refs_0_), channel_id=1, source_target_pairs={{0,24},{4,28},{8,0},{12,4},{16,8},{20,12},{24,16},{28,20},{1,25},{... | collective-permute-start | bytes 589832 | tf_op jit(solution)/shard_map/ppermute | solution.py:219
  99.8 33.1 %collective-permute-start.23 = (bf16[384,256]{1,0:T(8,128)(2,1)}, bf16[384,256]{1,0:T(8,128)(2,1)S(1)}, u32[]{:S(2)}, u32[]{:S(2)}) collective-permute-start(bf16[384,256]{1,0:T(8,128)(2,1)} %collective-permute-done.19.refs_1_), channel_id=1, source_target_pairs={{0,4},{4,0},{8,12},{12,8},{16,20},{20,16},{24,28},{28,24},{1,5},{5... | collective-permute-start | bytes 589832 | tf_op jit(solution)/shard_map/ppermute | solution.py:23
  99.9 30.3 %copy-start.24 = (bf16[384,256]{1,0:T(8,128)(2,1)}, bf16[384,256]{1,0:T(8,128)(2,1)S(1)}, u32[]{:S(2)}) copy-start(bf16[384,256]{1,0:T(8,128)(2,1)S(1)} %collective-permute-done.22.refs_4_) | copy-start | bytes 589828
  99.9 33.8 %collective-permute-start.24 = (bf16[384,256]{1,0:T(8,128)(2,1)}, bf16[384,256]{1,0:T(8,128)(2,1)}, u32[]{:S(2)}, u32[]{:S(2)}) collective-permute-start(bf16[384,256]{1,0:T(8,128)(2,1)} %collective-permute-done.20.refs_2_), channel_id=1, source_target_pairs={{0,4},{4,0},{8,12},{12,8},{16,20},{20,16},{24,28},{28,24},{1,5},{5... | collective-permute-start | bytes 589832 | tf_op jit(solution)/shard_map/ppermute | solution.py:23
  101.4 28.8 %copy-start.22 = (bf16[384,256]{1,0:T(8,128)(2,1)}, bf16[384,256]{1,0:T(8,128)(2,1)S(1)}, u32[]{:S(2)}) copy-start(bf16[384,256]{1,0:T(8,128)(2,1)S(1)} %collective-permute-done.26.refs_1_) | copy-start | bytes 589828
  101.4 33.8 %collective-permute-start.25 = (bf16[384,256]{1,0:T(8,128)(2,1)}, bf16[384,256]{1,0:T(8,128)(2,1)}, u32[]{:S(2)}, u32[]{:S(2)}) collective-permute-start(bf16[384,256]{1,0:T(8,128)(2,1)} %collective-permute-done.21.refs_3_), channel_id=1, source_target_pairs={{0,4},{4,0},{8,12},{12,8},{16,20},{20,16},{24,28},{28,24},{1,5},{5... | collective-permute-start | bytes 589832 | tf_op jit(solution)/shard_map/ppermute | solution.py:23
  130.2 4.9 %copy-start.10 = (f32[64,256]{1,0:T(8,128)}, f32[64,256]{1,0:T(8,128)S(1)}, u32[]{:S(2)}) copy-start(f32[64,256]{1,0:T(8,128)S(1)} %get-tuple-element.114) | copy-start | bytes 196612
  131.5 38.2 %collective-permute-start.29 = (bf16[384,256]{1,0:T(8,128)(2,1)}, bf16[384,256]{1,0:T(8,128)(2,1)S(1)}, u32[]{:S(2)}, u32[]{:S(2)}) collective-permute-start(bf16[384,256]{1,0:T(8,128)(2,1)} %get-tuple-element.100.refs_0_), channel_id=1, source_target_pairs={{0,4},{4,0},{8,12},{12,8},{16,20},{20,16},{24,28},{28,24},{1,5},{5... | collective-permute-start | bytes 589832 | tf_op jit(solution)/shard_map/ppermute | solution.py:23
  131.5 38.2 %collective-permute-start.30 = (bf16[384,256]{1,0:T(8,128)(2,1)}, bf16[384,256]{1,0:T(8,128)(2,1)S(1)}, u32[]{:S(2)}, u32[]{:S(2)}) collective-permute-start(bf16[384,256]{1,0:T(8,128)(2,1)} %copy-done.22), channel_id=1, source_target_pairs={{0,4},{4,0},{8,12},{12,8},{16,20},{20,16},{24,28},{28,24},{1,5},{5... | collective-permute-start | bytes 589832 | tf_op jit(solution)/shard_map/ppermute | solution.py:23
  133.6 36.0 %collective-permute-start.31 = (bf16[384,256]{1,0:T(8,128)(2,1)}, bf16[384,256]{1,0:T(8,128)(2,1)S(1)}, u32[]{:S(2)}, u32[]{:S(2)}) collective-permute-start(bf16[384,256]{1,0:T(8,128)(2,1)} %collective-permute-done.27.refs_2_), channel_id=1, source_target_pairs={{0,4},{4,0},{8,12},{12,8},{16,20},{20,16},{24,28},{28,24},{1,5},{5... | collective-permute-start | bytes 589832 | tf_op jit(solution)/shard_map/ppermute | solution.py:23
  133.7 36.0 %collective-permute-start.32 = (bf16[384,256]{1,0:T(8,128)(2,1)}, bf16[384,256]{1,0:T(8,128)(2,1)S(1)}, u32[]{:S(2)}, u32[]{:S(2)}) collective-permute-start(bf16[384,256]{1,0:T(8,128)(2,1)} %collective-permute-done.28.refs_3_), channel_id=1, source_target_pairs={{0,4},{4,0},{8,12},{12,8},{16,20},{20,16},{24,28},{28,24},{1,5},{5... | collective-permute-start | bytes 589832 | tf_op jit(solution)/shard_map/ppermute | solution.py:23
  135.1 0.9 copy-start.3
  136.9 1.9 copy-start.13
  138.8 0.9 copy-start.25
  140.6 29.1 %copy-start.23 = (bf16[384,256]{1,0:T(8,128)(2,1)S(1)}, bf16[384,256]{1,0:T(8,128)(2,1)}, u32[]{:S(2)}) copy-start(bf16[384,256]{1,0:T(8,128)(2,1)} %copy-done.22) | copy-start | bytes 589828
  169.6 29.8 %copy-start.6 = (bf16[256,128]{1,0:T(8,128)(2,1)}, bf16[256,128]{1,0:T(8,128)(2,1)S(1)}, u32[]{:S(2)}) copy-start(bf16[256,128]{1,0:T(8,128)(2,1)S(1)} %get-tuple-element.111) | copy-start | bytes 196612
  169.7 1.1 copy-start.1
  170.8 29.3 %copy-start.9 = (f32[64,256]{1,0:T(8,128)S(1)}, f32[64,256]{1,0:T(8,128)}, u32[]{:S(2)}) copy-start(f32[64,256]{1,0:T(8,128)} %copy-done.8) | copy-start | bytes 196612
  170.8 29.3 %copy-start.11 = (f32[64,256]{1,0:T(8,128)S(1)}, f32[64,256]{1,0:T(8,128)}, u32[]{:S(2)}) copy-start(f32[64,256]{1,0:T(8,128)} %copy-done.10) | copy-start | bytes 196612
  200.2 8.1 %collective-permute-start.34 = (f32[4,8,8,256]{3,2,1,0:T(8,128)S(1)}, f32[4,8,8,256]{3,2,1,0:T(8,128)}, u32[]{:S(2)}, u32[]{:S(2)}) collective-permute-start(f32[4,8,8,256]{3,2,1,0:T(8,128)S(1)} %pad_maximum_fusion.2), channel_id=1, source_target_pairs={{0,1},{1,0},{2,3},{3,2},{4,5},{5,4},{6,7},{7,6},{8,9},{9,8},{10,11... | collective-permute-start | bytes 786440 | tf_op jit(solution)/shard_map/ppermute | solution.py:23
  206.3 3.6 %collective-permute-start.33 = (bf16[4,8,4,1024]{3,2,1,0:T(4,128)(2,1)S(1)}, bf16[4,8,4,1024]{3,2,1,0:T(4,128)(2,1)S(1)}, u32[]{:S(2)}, u32[]{:S(2)}) collective-permute-start(bf16[4,8,4,1024]{3,2,1,0:T(4,128)(2,1)S(1)} %pad_maximum_fusion.1), channel_id=1, source_target_pairs={{0,1},{1,0},{2,3},{3,2},{4,5},{5,4},{6,7},{7,6},{8,9},{9,8},{10,11... | collective-permute-start | bytes 786440 | tf_op jit(solution)/shard_map/ppermute | solution.py:23
  (7 other events, 5.0 us)
